TPU v7x, 512 devices: a whole 4x4x16 slice. The times are simulated.
512 devices in a mesh: row: 32 (over z, core), col: 16 (over x, y).
Axes of the slice: x: 4, y: 4, z: 16, core: 2. Of those that a mesh axis runs over, the one named last changes fastest.
Arguments:
- locations: int32 [1, 16384], P(None, 'row'), may hold values from 0 to 65535, as said below
- scales: float32 [1, 16384], P(None, 'row'), may hold values from 0.5 to 2
- sample_times: int32 [1, 16384], P(None, 'row'), may hold values from 0 to 2047
Outputs:
- factored: bfloat16 [1, 16384, 2, 8192], P(None, 'row', None, 'col')
Inputs may be any that keep to these rules, and one draw needn't show every extreme that they name: `locations`: distinct Morton codes of cells of a 256 by 256 grid, increasing in row-major order; the first and last cells are always among them.
All inputs are finite; a program needn't handle non-finite values.
Results may differ from a plain program's by a relative error of at most 0.007.
Values may be sent and summed in bfloat16 or wider, within the bound.
No kernel may reach another device: no remote copies, remote signals or barrier semaphores. Data moves between devices by JAX's collectives and lax.ppermute only.
A program may use at most 64 MiB of HBM per device.

v0:
```python
import jax
import jax.numpy as jnp
from jax import lax
from jax.sharding import PartitionSpec as P

NB = 512
PANELS = 2
GRID = 256


RANGE_LENGTH = 0.3
TIME_RANGE = 8.0
NUGGET = 1.0


def spread(value, axis, source):
    kept = jnp.where(lax.axis_index(axis) == source, value, 0).astype(value.dtype)
    return lax.psum(kept, axis)


def decode_points(locations):
    bit_count = GRID.bit_length() - 1
    across = jnp.zeros_like(locations)
    upward = jnp.zeros_like(locations)
    for bit_level in range(bit_count):
        across = across + locations // 4**bit_level % 2 * 2**bit_level
        upward = upward + locations // (2 * 4**bit_level) % 2 * 2**bit_level
    return ((across.astype(jnp.float32) + 0.5) / GRID, (upward.astype(jnp.float32) + 0.5) / GRID)


def covariance(first, second, self_pairs):
    delta_x = first[0][..., :, None] - second[0][..., None, :]
    delta_y = first[1][..., :, None] - second[1][..., None, :]
    delta_t = first[2][..., :, None] - second[2][..., None, :]
    distance = jnp.sqrt(delta_x * delta_x + delta_y * delta_y)
    decay_term = jnp.exp(-(distance / RANGE_LENGTH + jnp.abs(delta_t) / TIME_RANGE))
    decay_term = jnp.where(self_pairs, decay_term + NUGGET, decay_term)
    return first[3][..., :, None] * second[3][..., None, :] * decay_term


def block_covariance(first, second):
    delta_x = first[0][:, None, None] - second[0][None, :, :]
    delta_y = first[1][:, None, None] - second[1][None, :, :]
    delta_t = first[2][:, None, None] - second[2][None, :, :]
    distance = jnp.sqrt(delta_x * delta_x + delta_y * delta_y)
    decay_term = jnp.exp(-(distance / RANGE_LENGTH + jnp.abs(delta_t) / TIME_RANGE))
    return first[3][:, None, None] * second[3][None, :, :] * decay_term


def product(left, right):
    return lax.dot_general(
        left, right, (((1,), (1,)), ((), ())), preferred_element_type=jnp.float32
    )


def solve_tiles(factor, raw_tiles, row_ids, panel_index):
    row_rounds = raw_tiles.shape[0]
    flattened = raw_tiles.reshape(row_rounds * NB, NB).astype(jnp.float32)
    solved = lax.linalg.triangular_solve(
        factor, flattened, left_side=False, lower=True, transpose_a=True
    )
    solved = solved.reshape(row_rounds, NB, NB)
    return jnp.where((row_ids > panel_index)[:, None, None], solved, 0.0).astype(jnp.bfloat16)


def apply_range(local_block, row_panel, column_panel, first_round, last_round):
    row_rounds = row_panel.shape[0]
    span_rounds = last_round - first_round
    change = product(
        row_panel.reshape(row_rounds * NB, NB), column_panel.reshape(span_rounds * NB, NB)
    )
    change = change.reshape(row_rounds, NB, span_rounds, NB)
    previous = local_block.astype(jnp.float32)
    return local_block.at[:, :, first_round:last_round, :].set(
        (previous - change).astype(jnp.bfloat16)
    )


def per_device(locations, scales, sample_times):
    row_rounds = locations.shape[0]
    row_size = lax.axis_size("row")
    col_size = lax.axis_size("col")
    tile_count = row_rounds * row_size
    col_rounds = tile_count // col_size
    row_place = lax.axis_index("row")
    col_place = lax.axis_index("col")
    across, upward = decode_points(locations)
    moments = sample_times.astype(jnp.float32)
    stacked = jnp.stack([across, upward, moments, scales])
    gathered = lax.all_gather(stacked, "row", axis=2, tiled=True)
    by_round = gathered.reshape(4, col_rounds, col_size, NB)
    my_columns = lax.dynamic_index_in_dim(by_round, col_place, 2, keepdims=False)
    own_points = (across, upward, moments, scales)
    col_points = (my_columns[0], my_columns[1], my_columns[2], my_columns[3])

    def generate(round_points):
        return block_covariance(round_points, col_points).astype(jnp.bfloat16)

    local_block = lax.map(generate, own_points)
    self_pairs = (
        jnp.arange(NB, dtype=jnp.int32)[:, None] == jnp.arange(NB, dtype=jnp.int32)[None, :]
    )[None]
    diagonal = covariance(own_points, own_points, self_pairs)
    row_ids = row_place + row_size * jnp.arange(row_rounds, dtype=jnp.int32)
    col_ids = col_place + col_size * jnp.arange(col_rounds, dtype=jnp.int32)
    deferred = None
    for panel_index in range(PANELS):
        owner_row = panel_index % row_size
        local_row = panel_index // row_size
        owner_col = panel_index % col_size
        local_col = panel_index // col_size
        arriving = spread(diagonal[local_row].astype(jnp.bfloat16), "row", owner_row).astype(
            jnp.float32
        )
        factor = jnp.linalg.cholesky(arriving)
        solved_here = solve_tiles(factor, local_block[:, :, local_col, :], row_ids, panel_index)
        row_panel = spread(solved_here, "col", owner_col)

        def fetch(position, collected):
            wanted = col_place + col_size * position
            picked_tile = lax.dynamic_index_in_dim(row_panel, wanted // row_size, 0, keepdims=False)
            arrived = spread(picked_tile, "row", wanted % row_size)
            return lax.dynamic_update_index_in_dim(collected, arrived, position, 0)

        column_panel = lax.fori_loop(
            0, col_rounds, fetch, jnp.zeros((col_rounds, NB, NB), jnp.bfloat16)
        )
        diagonal = diagonal.at[local_row].set(
            jnp.where(row_place == owner_row, factor, diagonal[local_row])
        )
        current = local_block[:, :, local_col, :]
        local_block = local_block.at[:, :, local_col, :].set(
            jnp.where(col_place == owner_col, row_panel, current)
        )
        above_band = (row_place == owner_row) & (col_ids > panel_index)
        band_rows = local_block[local_row]
        local_block = local_block.at[local_row].set(
            jnp.where(above_band[None, :, None], jnp.zeros_like(band_rows), band_rows)
        )
        diagonal = diagonal - jnp.einsum(
            "anx,amx->anm", row_panel, row_panel, preferred_element_type=jnp.float32
        )
        local_block = apply_range(local_block, row_panel, column_panel, 0, col_rounds)
    diagonal_round = row_ids // col_size
    holds_diagonal = (row_ids % col_size == col_place)[:, None] & (
        jnp.arange(col_rounds, dtype=jnp.int32)[None, :] == diagonal_round[:, None]
    )
    local_block = jnp.where(
        holds_diagonal[:, None, :, None], diagonal[:, :, None, :].astype(jnp.bfloat16), local_block
    )
    return local_block


def solution(mesh):
    return jax.shard_map(
        per_device,
        mesh=mesh,
        in_specs=(P(None, "row"), P(None, "row"), P(None, "row")),
        out_specs=P(None, "row", None, "col"),
        check_vma=False,
    )
```

profile of v0, /device:TPU:1, one launch (start us, length us, event | category | flops | bytes accessed | tf_op | source)
XLA Modules:
  0.0 1843.2 jit_solution(9361769270682796442)
XLA Ops:
  8.1 2.6 convert_select_fusion.1
  12.1 38.3 %all_gather.3 = f32[4,1,16384]{2,0,1:T(4,128)S(1)} all-gather(f32[4,1,512]{2,0,1:T(4,128)S(1)} %pad_maximum_fusion), channel_id=1, replica_groups=mesh['row'=32,'col'=16] {'row'}, dimensions={2}, use_global_device_ids=true | all-gather | bytes 270336 | tf_op jit(solution)/shard_map/all_gather | solution.py:90
  51.7 1.1 bitcast_convert_fusion.1
  52.8 171.6 %all-reduce.8.cloned.1.call-done = bf16[512,512]{0,1:T(8,128)(2,1)} async-done(((bf16[512,512]{0,1:T(8,128)(2,1)}), bf16[512,512]{0,1:T(8,128)(2,1)}) %all-reduce.8.cloned.1.call-update) | async-done | bytes 524304 | tf_op jit(solution)/shard_map/psum | solution.py:18
  224.4 1.3 copy.31
  225.7 1.2 fusion.12
  226.9 11.7 cholesky.286
  239.4 9.8 custom-call.27
  250.0 12.2 cholesky.305
  263.4 10.4 custom-call.28
  275.7 1.2 convolution_dynamic-update-slice_fusion.1
  277.5 11.7 cholesky.326
  289.3 9.8 custom-call.29
  299.9 11.9 cholesky.343
  313.3 1.3 compare_reduce_fusion.6
  317.3 8.8 while.50
  318.0 1.4 dynamic-slice.75
  320.2 1.4 dynamic-slice.75
  322.4 1.4 dynamic-slice.75
  324.6 1.4 dynamic-slice.75
  326.8 40.1 %custom-call.30 = f32[4,128,128]{1,2,0:T(8,128)S(1)} custom-call(f32[4,128,128]{2,1,0:T(8,128)} %copy-done.6), custom_call_target="InvertDiagBlocksLowerTriangular" | custom-call | tf_op jit(solution)/shard_map/triangular_solve/custom-call.3 | solution.py:59
  371.3 2.5 multiply_convert_fusion
  373.8 111.8 %all-reduce.10.cloned.1.call-done = bf16[1,512,512]{1,2,0:T(8,128)(2,1)} async-done(((bf16[1,512,512]{1,2,0:T(8,128)(2,1)}), bf16[1,512,512]{1,2,0:T(8,128)(2,1)}) %all-reduce.10.cloned.1.call-update) | async-done | bytes 524304 | tf_op jit(solution)/shard_map/psum | solution.py:18
  485.6 1.3 copy.50
  486.9 3.6 convert_select_fusion
  490.6 425.2 %while.48 = (s32[]{:T(128)}, bf16[2,512,512]{2,1,0:T(8,128)(2,1)S(1)}, s32[]{:T(128)}, bf16[1,512,512]{2,1,0:T(8,128)(2,1)S(1)}, s32[]{:T(128)}, /*index=5*/u32[...) while((s32[]{:T(128)}, bf16[2,512,512]{2,1,0:T(8,128)(2,1)S(1)}, s32[]{:T(128)}, ...), condition=%wide.region_13.16_spmd, body=%wide.region_11.15_spmd.sunk | while | flops 524307 | bytes 5243216 | solution.py:125
  491.5 211.2 %all-reduce.16.cloned.1.call-done = bf16[1,512,512]{2,1,0:T(8,128)(2,1)} async-done(((bf16[1,512,512]{2,1,0:T(8,128)(2,1)}), bf16[1,512,512]{2,1,0:T(8,128)(2,1)}) %all-reduce.16.cloned.1.call-update) | async-done | bytes 524304 | tf_op jit(solution)/shard_map/while/body/eval_jaxpr/psum | solution.py:18
  702.7 1.1 constant_dynamic-update-slice_fusion.12
  704.7 210.0 %all-reduce.16.cloned.1.call-done = bf16[1,512,512]{2,1,0:T(8,128)(2,1)} async-done(((bf16[1,512,512]{2,1,0:T(8,128)(2,1)}), bf16[1,512,512]{2,1,0:T(8,128)(2,1)}) %all-reduce.16.cloned.1.call-update) | async-done | bytes 524304 | tf_op jit(solution)/shard_map/while/body/eval_jaxpr/psum | solution.py:18
  914.8 1.1 constant_dynamic-update-slice_fusion.12
  917.6 1.9 subtract_convert_fusion.1
  919.7 207.1 %all-reduce.12.cloned.1.call-done = bf16[512,512]{0,1:T(8,128)(2,1)} async-done(((bf16[512,512]{0,1:T(8,128)(2,1)}), bf16[512,512]{0,1:T(8,128)(2,1)}) %all-reduce.12.cloned.1.call-update) | async-done | bytes 524304 | tf_op jit(solution)/shard_map/psum | solution.py:18
  1126.8 1.3 copy.41
  1128.1 1.2 fusion.11
  1130.3 11.7 cholesky.358
  1142.7 9.8 custom-call.31
  1152.5 1.2 fusion.48
  1153.9 1.3 convolution_subtract_fusion.8
  1155.2 11.7 cholesky.377
  1167.7 10.8 custom-call.32
  1180.3 1.2 convolution_dynamic-update-slice_fusion
  1181.5 1.5 convolution_subtract_fusion.10
  1183.0 11.7 cholesky.398
  1194.8 9.8 custom-call.33
  1205.0 1.3 convolution_subtract_fusion.12
  1206.3 11.9 cholesky.415
  1223.5 1.1 fusion.13
  1224.6 12.2 while.51
  1225.3 2.2 dynamic-slice.77
  1228.3 2.2 dynamic-slice.77
  1231.4 2.2 dynamic-slice.77
  1234.5 2.2 dynamic-slice.77
  1237.5 40.1 %custom-call.34 = f32[4,128,128]{1,2,0:T(8,128)S(1)} custom-call(f32[4,128,128]{2,1,0:T(8,128)} %copy-done.5), custom_call_target="InvertDiagBlocksLowerTriangular" | custom-call | tf_op jit(solution)/shard_map/triangular_solve/custom-call.3 | solution.py:59
  1278.0 1.2 convolution_subtract_fusion.3
  1279.7 1.4 convolution_subtract_fusion.2
  1281.5 1.6 convolution_subtract_fusion.6
  1285.6 113.4 %all-reduce.14.cloned.1.call-done = bf16[1,512,512]{1,2,0:T(8,128)(2,1)} async-done(((bf16[1,512,512]{1,2,0:T(8,128)(2,1)}), bf16[1,512,512]{1,2,0:T(8,128)(2,1)}) %all-reduce.14.cloned.1.call-update) | async-done | bytes 524304 | tf_op jit(solution)/shard_map/psum | solution.py:18
  1399.0 1.3 copy.54
  1401.2 1.3 fusion.2
  1402.6 427.0 %while.49 = (s32[]{:T(128)}, bf16[2,512,512]{2,1,0:T(8,128)(2,1)S(1)}, s32[]{:T(128)}, bf16[1,512,512]{2,1,0:T(8,128)(2,1)S(1)}, s32[]{:T(128)}, /*index=5*/u32[...) while((s32[]{:T(128)}, bf16[2,512,512]{2,1,0:T(8,128)(2,1)S(1)}, s32[]{:T(128)}, ...), condition=%wide.region_17.20_spmd, body=%wide.region_15.19_spmd.sunk | while | flops 524307 | bytes 5243216 | solution.py:125
  1403.6 212.5 %all-reduce.18.cloned.1.call-done = bf16[1,512,512]{2,1,0:T(8,128)(2,1)} async-done(((bf16[1,512,512]{2,1,0:T(8,128)(2,1)}), bf16[1,512,512]{2,1,0:T(8,128)(2,1)}) %all-reduce.18.cloned.1.call-update) | async-done | bytes 524304 | tf_op jit(solution)/shard_map/while/body/eval_jaxpr/psum | solution.py:18
  1618.1 210.4 %all-reduce.18.cloned.1.call-done = bf16[1,512,512]{2,1,0:T(8,128)(2,1)} async-done(((bf16[1,512,512]{2,1,0:T(8,128)(2,1)}), bf16[1,512,512]{2,1,0:T(8,128)(2,1)}) %all-reduce.18.cloned.1.call-update) | async-done | bytes 524304 | tf_op jit(solution)/shard_map/while/body/eval_jaxpr/psum | solution.py:18
  1829.6 2.9 fusion.1
  1832.5 3.7 copy.57
  (173 shorter events, 43.6 us)
Async XLA Ops:
  6.5 217.9 %all-reduce.8.cloned.1.call-start = ((), (), s32[]{:S(2)}) async-start(), calls=%async_computation | async-start | bytes 1048576 | tf_op jit(solution)/shard_map/psum | solution.py:18
  7.2 43.5 %copy-start.13 = (f32[1,512]{1,0:T(1,128)}, f32[1,512]{1,0:T(1,128)S(1)}, u32[]{:S(2)}) copy-start(f32[1,512]{1,0:T(1,128)S(1)} %get-tuple-element.477) | copy-start | bytes 6148
  10.7 474.9 %all-reduce.10.cloned.1.call-start = ((), (), s32[]{:S(2)}) async-start(), calls=%async_computation.1 | async-start | bytes 1048576 | tf_op jit(solution)/shard_map/psum | solution.py:18
  50.5 1.2 copy-start.7
  50.5 1.2 copy-start.15
  50.8 0.9 copy-start.9
  50.8 0.9 copy-start.11
  276.8 40.4 %copy-start.17 = (s32[4]{0:T(128)S(1)}, s32[4]{0:T(128)}, u32[]{:S(2)}) copy-start(s32[4]{0:T(128)} %iota_multiply_fusion) | copy-start | bytes 52
  326.1 0.7 copy-start.6
  369.1 2.1 copy-start.8
  369.1 2.1 copy-start.10
  369.1 2.1 copy-start.12
  369.1 2.1 copy-start.14
  369.2 2.1 copy-start.16
  490.6 426.1 %copy-start.2 = (bf16[1,512,512]{1,2,0:T(8,128)(2,1)S(1)}, bf16[1,512,512]{1,2,0:T(8,128)(2,1)}, u32[]{:S(2)}) copy-start(bf16[1,512,512]{1,2,0:T(8,128)(2,1)} %all-reduce.10.cloned.1.call-done) | copy-start | bytes 1572868
  490.6 426.1 %copy-start.3 = (bf16[1,512,1,512]{1,3,2,0:T(8,128)(2,1)S(1)}, bf16[1,512,1,512]{1,3,2,0:T(8,128)(2,1)}, u32[]{:S(2)}) copy-start(bf16[1,512,1,512]{1,3,2,0:T(8,128)(2,1)} %get-tuple-element.456) | copy-start | bytes 1572868
  490.6 212.1 %all-reduce.16.cloned.1.call-start = ((), (), s32[]{:S(2)}) async-start(), calls=%async_computation.4 | async-start | bytes 1048576 | tf_op jit(solution)/shard_map/while/body/eval_jaxpr/psum | solution.py:18
  703.8 211.0 %all-reduce.16.cloned.1.call-start = ((), (), s32[]{:S(2)}) async-start(), calls=%async_computation.4 | async-start | bytes 1048576 | tf_op jit(solution)/shard_map/while/body/eval_jaxpr/psum | solution.py:18
  915.8 211.0 %all-reduce.12.cloned.1.call-start = ((), (), s32[]{:S(2)}) async-start(), calls=%async_computation.2 | async-start | bytes 1048576 | tf_op jit(solution)/shard_map/psum | solution.py:18
  916.4 482.5 %all-reduce.14.cloned.1.call-start = ((), (), s32[]{:S(2)}) async-start(), calls=%async_computation.3 | async-start | bytes 1048576 | tf_op jit(solution)/shard_map/psum | solution.py:18
  1129.3 1.0 copy-start
  1236.8 0.7 copy-start.5
  1399.0 2.3 copy-start.1
  1402.6 427.0 %copy-start.4 = (bf16[512,2,512]{0,2,1:T(8,128)(2,1)S(1)}, bf16[512,2,512]{0,2,1:T(8,128)(2,1)}, u32[]{:S(2)}) copy-start(bf16[512,2,512]{0,2,1:T(8,128)(2,1)} %bitcast_dynamic-update-slice_fusion.2) | copy-start | bytes 3145732
  1402.6 213.4 %all-reduce.18.cloned.1.call-start = ((), (), s32[]{:S(2)}) async-start(), calls=%async_computation.5 | async-start | bytes 1048576 | tf_op jit(solution)/shard_map/while/body/eval_jaxpr/psum | solution.py:18
  1617.1 211.4 %all-reduce.18.cloned.1.call-start = ((), (), s32[]{:S(2)}) async-start(), calls=%async_computation.5 | async-start | bytes 1048576 | tf_op jit(solution)/shard_map/while/body/eval_jaxpr/psum | solution.py:18
Sparse Core Ops, SparseCore 0:
  10.9 213.5 all-reduce.7
  371.3 114.2 all-reduce.9
  493.8 208.8 all-reduce.15
  706.6 208.0 all-reduce.15
  918.7 208.0 all-reduce.11
  1284.6 114.2 all-reduce.13
  1405.9 210.0 all-reduce.17
  1620.4 208.0 all-reduce.17
where the time goes:
time: 1850 us; the launch traced here: 1840 us
  waiting for transfers between devices  1450 us (78%)
  other arithmetic  262 us (14%)
  local copies, waits for them, and re-layouts  44.7 us (2%)
  blocking collectives  38.3 us (2%)
  matrix products  28.8 us (2%)
  between operations  19.5 us (1%)
    psum x8, waiting for transfers between devices, spread(): return lax.psum(kept, axis)  1450 us
    another operation x29, other arithmetic, per_device(): factor = jnp.linalg.cholesky(arriving)  161 us
    another operation x5, other arithmetic, solve_tiles(): lax.linalg.triangular_solve(factor, flattened, left_side=False, lower=Tru...  82.1 us
    all_gather x1, blocking collectives, per_device(): gathered = lax.all_gather(stacked, 'row', axis=2, tiled=True)  38.3 us
  transfers between devices with their start and end apart: 8, of which 8 were waited for; matrix products, arithmetic and copies ran while one was open for 1% of the time, Pallas kernels for 0%

commit v1 on v0

v1 whole, which is shorter than its diff:
```python
import functools

import jax
import jax.numpy as jnp
from jax import lax
from jax.experimental import pallas as pl
from jax.experimental.pallas import tpu as pltpu
from jax.sharding import PartitionSpec as P

NB = 512
BLOCK = 128
STEP = 16
PANELS = 2
GRID = 256
RANGE_LENGTH = 0.3
TIME_RANGE = 8.0
NUGGET = 1.0
LOG2E = 1.4426950408889634
HIGH = lax.Precision.HIGH
F32 = jnp.float32
BF16 = jnp.bfloat16


def dot_nt(a, b, precision=None):
    return lax.dot_general(
        a, b, (((1,), (1,)), ((), ())), preferred_element_type=F32, precision=precision
    )


def dot_nn(a, b, precision=None):
    return lax.dot_general(
        a, b, (((1,), (0,)), ((), ())), preferred_element_type=F32, precision=precision
    )


def lane_column(value, column):
    return jnp.broadcast_to(value[:, column : column + 1], (8, BLOCK))


def sublane_row(value, row):
    return jnp.broadcast_to(value[row : row + 1, :], (8, BLOCK))


def inverse_factor(block):
    groups = BLOCK // 8
    sub = lax.broadcasted_iota(jnp.int32, (8, BLOCK), 0)
    lane = lax.broadcasted_iota(jnp.int32, (8, BLOCK), 1)
    unit = [jnp.where(sub == r, 1.0, 0.0).astype(F32) for r in range(8)]
    rows = [block[8 * g : 8 * g + 8, :] for g in range(groups)]
    result = []
    for step in range(BLOCK // STEP):
        first = step * STEP
        top = first // 8
        inside = (lane >= first) & (lane < first + STEP)
        columns = [[lane_column(rows[top + a], first + c) for a in range(2)] for c in range(STEP)]
        pivot = [
            jnp.where(inside, jnp.where(lane - first == sub + 8 * a, 1.0, 0.0), rows[top + a])
            for a in range(2)
        ]
        done = [jnp.zeros((8, BLOCK), F32), jnp.zeros((8, BLOCK), F32)]
        for pair in range(STEP // 2):
            c0, c1 = 2 * pair, 2 * pair + 1
            a, r0, r1 = c0 // 8, c0 % 8, c1 % 8
            d00 = sublane_row(columns[c0][a], r0)
            d01 = sublane_row(columns[c1][a], r0)
            d11 = sublane_row(columns[c1][a], r1)
            scale = 1.0 / (d00 * d11 - d01 * d01)
            w0 = [columns[c0][g] - unit[r0] if g == a else columns[c0][g] for g in range(2)]
            w1 = [columns[c1][g] - unit[r1] if g == a else columns[c1][g] for g in range(2)]

            def sweep(z):
                z0, z1 = sublane_row(z[a], r0), sublane_row(z[a], r1)
                y0 = (d11 * z0 - d01 * z1) * scale
                y1 = (d00 * z1 - d01 * z0) * scale
                return [z[g] - (w0[g] * y0 + w1[g] * y1) for g in range(2)], z0, z1

            for c in range(c1 + 1, STEP):
                columns[c], _, _ = sweep(columns[c])
            pivot, z0, z1 = sweep(pivot)
            ratio = d01 / d00
            x0 = z0 * lax.rsqrt(d00)
            x1 = (z1 - z0 * ratio) * lax.rsqrt(d11 - d01 * ratio)
            done[a] = jnp.where(sub == r0, x0, jnp.where(sub == r1, x1, done[a]))
        result += done
        if step == BLOCK // STEP - 1:
            break
        near = range(top + 2, top + 4)
        old = list(rows)
        for h in near:
            total = jnp.where(inside, 0.0, old[h])
            parts = [
                lane_column(old[h], first + c) * sublane_row(pivot[c // 8], c % 8)
                for c in range(STEP)
            ]
            while len(parts) > 1:
                parts = [parts[i] + parts[i + 1] for i in range(0, len(parts), 2)]
            rows[h] = total - parts[0]
        if top + 4 < groups:
            below = jnp.concatenate(old[top + 4 :], axis=0)
            spread = jnp.concatenate(
                ([jnp.zeros((first, BLOCK), F32)] if first else [])
                + pivot
                + [jnp.zeros((BLOCK - first - STEP, BLOCK), F32)],
                axis=0,
            )
            change = dot_nn(below, spread, HIGH)
            for h in range(top + 4, groups):
                k = h - top - 4
                rows[h] = jnp.where(inside, 0.0, old[h]) - change[8 * k : 8 * k + 8, :]
    out = jnp.concatenate(result, axis=0)
    r = lax.broadcasted_iota(jnp.int32, (BLOCK, BLOCK), 0)
    c = lax.broadcasted_iota(jnp.int32, (BLOCK, BLOCK), 1)
    return jnp.where(c <= r, out, 0.0)


def tile_kernel(
    place_ref, gathered_ref, out_ref,
    lanes, subs, schur, lower, inverse, high, low, current, unit_inverse, factors,
    first_panel, cov, panels,
):
    row_tile = place_ref[0]
    col_tile = place_ref[1]
    second_col = place_ref[2]
    ids = (0, 1, row_tile, col_tile, second_col)

    for slot, tile in enumerate(ids):
        raw = gathered_ref[tile]
        codes = raw[0:1, :].astype(jnp.int32)
        across = jnp.zeros_like(codes)
        upward = jnp.zeros_like(codes)
        for bit in range(GRID.bit_length() - 1):
            across = across + (((codes >> (2 * bit)) & 1) << bit)
            upward = upward + (((codes >> (2 * bit + 1)) & 1) << bit)
        step = LOG2E / (RANGE_LENGTH * GRID)
        x = across.astype(F32) * step
        y = upward.astype(F32) * step
        t = raw[1:2, :] * (LOG2E / TIME_RANGE)
        s = raw[2:3, :]
        stacked = jnp.concatenate([x, y, t, s, jnp.zeros((4, NB), F32)], axis=0)
        lanes[:, slot * NB : (slot + 1) * NB] = stacked
        for q in range(NB // BLOCK):
            part = stacked[:, q * BLOCK : (q + 1) * BLOCK]
            subs[slot * NB + q * BLOCK : slot * NB + (q + 1) * BLOCK, :] = part.T

    def covariance(row_start, row_count, col_start):
        rows = pl.ds(row_start, row_count)
        cols = pl.ds(col_start, NB)
        dx = subs[rows, 0:1] - lanes[0:1, cols]
        dy = subs[rows, 1:2] - lanes[1:2, cols]
        dt = subs[rows, 2:3] - lanes[2:3, cols]
        square = dx * dx + dy * dy
        length = square * lax.rsqrt(jnp.maximum(square, 1e-30))
        decay = jnp.exp2(-(length + jnp.abs(dt)))
        return decay, subs[rows, 3:4] * lanes[3:4, cols]

    def own_pairs(start, count):
        r = lax.broadcasted_iota(jnp.int32, (count, NB), 0) + start
        c = lax.broadcasted_iota(jnp.int32, (count, NB), 1)
        return r == c

    chunk = 64

    def fill_offdiagonal(row_slot, col_slot):
        @pl.loop(0, NB // chunk)
        def _(i):
            start = pl.multiple_of(i * chunk, chunk)
            decay, gain = covariance(
                pl.multiple_of(row_slot * NB + start, chunk), chunk, col_slot * NB
            )
            cov[pl.ds(start, chunk), :] = (decay * gain).astype(BF16)

    def fill_diagonal(slot, change):
        @pl.loop(0, NB // chunk)
        def _(i):
            start = pl.multiple_of(i * chunk, chunk)
            decay, gain = covariance(
                pl.multiple_of(slot * NB + start, chunk), chunk, slot * NB
            )
            decay = jnp.where(own_pairs(start, chunk), decay + NUGGET, decay)
            value = decay * gain
            if change:
                value = value - schur[pl.ds(start, chunk), :]
            schur[pl.ds(start, chunk), :] = value

    def solve(values, panel):
        half = NB // 2
        left = values[:, :half]
        parts = [
            dot_nt(left, high[panel, :half, :half]) + dot_nt(left, low[panel, :half, :half]),
            dot_nt(values, high[panel, half:, :]) + dot_nt(values, low[panel, half:, :]),
        ]
        return jnp.concatenate(parts, axis=1).astype(BF16)

    fill_diagonal(0, False)
    current[...] = schur[0:BLOCK, 0:BLOCK]
    factors[...] = jnp.zeros_like(factors)
    is_factor = (row_tile == col_tile) & (row_tile < PANELS)

    def stage(panel, part):
        begin, end = part * BLOCK, (part + 1) * BLOCK
        inv = unit_inverse[...]
        inverse[begin:end, begin:end] = inv

        @pl.when(is_factor & (row_tile == panel))
        def _():
            factors[begin:end, begin:end] = dot_nt(current[...], inv, HIGH).astype(BF16)

        if end < NB:
            solved = dot_nt(schur[end:, begin:end], inv, HIGH)
            lower[end:, begin:end] = solved

            @pl.when(is_factor & (row_tile == panel))
            def _():
                factors[end:, begin:end] = solved.astype(BF16)

            top = solved[:BLOCK]
            current[...] = schur[end : end + BLOCK, end : end + BLOCK] - dot_nt(top, top, HIGH)
            for q in range(end, NB, BLOCK):
                here = solved[q - end : q - end + BLOCK]
                schur[q:, q : q + BLOCK] = schur[q:, q : q + BLOCK] - dot_nt(
                    solved[q - end :], here, HIGH
                )
        else:
            half = NB // 2
            for q in (0, half):
                m = q + BLOCK
                e = q + half
                inverse[m:e, q:m] = -dot_nn(
                    inverse[m:e, m:e], dot_nn(lower[m:e, q:m], inverse[q:m, q:m], HIGH), HIGH
                )
                inverse[q:m, m:e] = jnp.zeros((BLOCK, BLOCK), F32)
            inverse[half:, :half] = -dot_nn(
                inverse[half:, half:], dot_nn(lower[half:, :half], inverse[:half, :half], HIGH), HIGH
            )
            inverse[:half, half:] = jnp.zeros((half, half), F32)
            whole = inverse[...]
            head = whole.astype(BF16)
            high[panel] = head
            low[panel] = (whole - head.astype(F32)).astype(BF16)
            if panel + 1 < PANELS:
                fill_offdiagonal(1, 0)
                solved = solve(cov[...], 0)
                first_panel[...] = solved
                schur[...] = dot_nt(solved, solved)
                fill_diagonal(1, True)
                current[...] = schur[0:BLOCK, 0:BLOCK]

    parts = NB // BLOCK

    @pl.loop(0, PANELS * parts)
    def _(index):
        unit_inverse[...] = inverse_factor(current[...])
        for k in range(PANELS * parts):
            pl.when(index == k)(functools.partial(stage, k // parts, k % parts))

    @pl.loop(0, 3)
    def _(k):
        slot = 2 + k
        place = pl.ds(pl.multiple_of(k * NB, NB), NB)
        fill_offdiagonal(slot, 0)
        solved = solve(cov[...], 0)
        panels[0, place, :] = solved
        fill_offdiagonal(slot, 1)
        reduced = (cov[...].astype(F32) - dot_nt(solved, first_panel[...])).astype(BF16)
        panels[1, place, :] = solve(reduced, 1)

    for k in range(2):
        tile = ids[3 + k]

        @pl.when((row_tile < PANELS) & (tile > row_tile))
        def _():
            out_ref[k] = jnp.zeros((NB, NB), BF16)

        @pl.when((row_tile >= PANELS) & (tile >= PANELS))
        def _():
            col_place = pl.ds((1 + k) * NB, NB)

            @pl.loop(0, NB // BLOCK)
            def _(i):
                start = pl.multiple_of(i * BLOCK, BLOCK)
                decay, gain = covariance(
                    pl.multiple_of(2 * NB + start, BLOCK), BLOCK, (3 + k) * NB
                )
                held = tile == row_tile
                decay = jnp.where(own_pairs(start, BLOCK) & held, decay + NUGGET, decay)
                value = decay * gain

                def kept(v):
                    return jnp.where(held, v, v.astype(BF16).astype(F32))

                value = kept(value)
                for panel in range(PANELS):
                    change = dot_nt(panels[panel, pl.ds(start, BLOCK), :], panels[panel, col_place, :])
                    value = kept(value - change)
                out_ref[k, pl.ds(start, BLOCK), :] = value.astype(BF16)

    for panel in range(PANELS):

        @pl.when((col_tile == panel) & (row_tile > panel))
        def _():
            out_ref[0] = panels[panel, 0:NB, :]

    @pl.when(is_factor)
    def _():
        r = lax.broadcasted_iota(jnp.int32, (NB, NB), 0)
        c = lax.broadcasted_iota(jnp.int32, (NB, NB), 1)
        out_ref[0] = jnp.where(c <= r, factors[...].astype(F32), 0.0).astype(BF16)


def device_tiles(place, gathered):
    vmem = pl.BlockSpec(memory_space=pltpu.VMEM)
    return pl.pallas_call(
        tile_kernel,
        out_shape=jax.ShapeDtypeStruct((2, NB, NB), BF16),
        in_specs=[pl.BlockSpec(memory_space=pltpu.SMEM), vmem],
        out_specs=vmem,
        scratch_shapes=[
            pltpu.VMEM((8, 5 * NB), F32),
            pltpu.VMEM((5 * NB, 8), F32),
            pltpu.VMEM((NB, NB), F32),
            pltpu.VMEM((NB, NB), F32),
            pltpu.VMEM((NB, NB), F32),
            pltpu.VMEM((PANELS, NB, NB), BF16),
            pltpu.VMEM((PANELS, NB, NB), BF16),
            pltpu.VMEM((BLOCK, BLOCK), F32),
            pltpu.VMEM((BLOCK, BLOCK), F32),
            pltpu.VMEM((NB, NB), BF16),
            pltpu.VMEM((NB, NB), BF16),
            pltpu.VMEM((NB, NB), BF16),
            pltpu.VMEM((PANELS, 3 * NB, NB), BF16),
        ],
        compiler_params=pltpu.CompilerParams(vmem_limit_bytes=48 * 1024 * 1024),
    )(place, gathered)


def per_device(locations, scales, sample_times):
    row_place = lax.axis_index("row")
    col_place = lax.axis_index("col")
    own = jnp.stack([locations.astype(F32), sample_times.astype(F32), scales], axis=1)
    gathered = lax.all_gather(own, "row", axis=0, tiled=True)
    place = jnp.stack([row_place, col_place, col_place + lax.axis_size("col")]).astype(jnp.int32)
    tiles = device_tiles(place, gathered)
    return jnp.transpose(tiles, (1, 0, 2))[None]


def solution(mesh):
    return jax.shard_map(
        per_device,
        mesh=mesh,
        in_specs=(P(None, "row"), P(None, "row"), P(None, "row")),
        out_specs=P(None, "row", None, "col"),
        check_vma=False,
    )
```

time: 1850 us -> 89.3 us (0.05)
  waiting for transfers between devices: 1450 us -> 0 us
  other arithmetic: 262 us -> 0.09 us
  Pallas kernels: 0 us -> 46.5 us
  local copies, waits for them, and re-layouts: 44.7 us -> 3.35 us
  matrix products: 28.8 us -> 0 us
  between operations: 19.5 us -> 0.02 us
    psum x8 -> x0, waiting for transfers between devices: 1450 us -> none  [spread(): return lax.psum(kept, axis)]
    another operation x35 -> x3, other arithmetic: 244 us -> 0.09 us  [the longest x1 0.08 us: per_device(): jnp.stack([row_place, col_place, col_place + lax.axis_size('col')])]
    pallas_call x0 -> x1, Pallas kernels: none -> 46.5 us  [device_tiles(): pl.pallas_call(tile_kernel, out_shape=jax.ShapeDtypeStruct((2, NB, NB), B...]
    another operation x71 -> x0, local copies, waits for them, and re-layouts: 28.1 us -> none  [the longest x43 20.7 us: solve_tiles(): lax.linalg.triangular_solve(factor, flattened, left_side=False, lower=Tru...]
    another operation x26 -> x0, matrix products: 19.1 us -> none  [the longest x12 9.93 us: per_device(): factor = jnp.linalg.cholesky(arriving)]
  transfers between devices with their start and end apart: 8 -> 0, of which waited for: 8 -> 0; matrix products, arithmetic and copies ran while one was open for 1% -> 0% of each run, Pallas kernels for 0% -> 0%
where the time goes in v1:
time: 89.3 us; the launch traced here: 88.2 us
  Pallas kernels  46.5 us (52%)
  blocking collectives  38.3 us (43%)
  local copies, waits for them, and re-layouts  3.35 us (4%)
    pallas_call x1, Pallas kernels, device_tiles(): pl.pallas_call(tile_kernel, out_shape=jax.ShapeDtypeStruct((2, NB, NB), B...  46.5 us
    all_gather x1, blocking collectives, per_device(): gathered = lax.all_gather(own, 'row', axis=0, tiled=True)  38.3 us
    broadcast_in_dim x1, local copies, waits for them, and re-layouts, per_device(): return jnp.transpose(tiles, (1, 0, 2))[None]  2.05 us

profile of v1, /device:TPU:1, one launch (start us, length us, event | category | flops | bytes accessed | tf_op | source)
XLA Modules:
  0.0 88.2 jit_solution(3719451405529831999)
XLA Ops:
  0.0 0.0 copy-start.2
  0.0 0.0 copy-start.1
  0.0 0.1 pad_add_fusion.place_ref
  0.1 0.6 copy-done.2
  0.7 0.0 copy-done.1
  0.7 0.0 copy-start
  0.7 0.7 copy-done
  1.4 38.3 %all_gather.3.gathered_ref = f32[32,3,512]{2,1,0:T(4,128)S(1)} all-gather(f32[1,3,512]{2,1,0:T(4,128)S(1)} %pad_maximum_fusion), channel_id=1, replica_groups=mesh['row'=32,'col'=16] {'row'}, dimensions={0}, use_global_device_ids=true | all-gather | bytes 202752 | tf_op jit(solution)/shard_map/all_gather | solution.py:340
  39.7 46.5 %shard_map.37 = bf16[2,512,512]{2,1,0:T(8,128)(2,1)S(1)} custom-call(s32[3]{0:T(128)S(1)} %pad_add_fusion.place_ref, f32[32,3,512]{2,1,0:T(4,128)S(1)} %all_gather.3.gathered_ref), custom_call_target="tpu_custom_call" | custom-call | tf_op jit(solution)/shard_map/pallas_call | solution.py:312
  86.2 2.0 %copy.5 = bf16[1,512,2,512]{3,2,1,0:T(2,128)(2,1)} copy(bf16[1,512,2,512]{3,1,2,0:T(8,128)(2,1)S(1)} %bitcast.11) | data formatting | bytes 2097152 | tf_op jit(solution)/shard_map/broadcast_in_dim | solution.py:343
  (2 shorter events, 0.0 us)
Async XLA Ops:
  0.0 0.7 copy-start.2
  0.0 0.7 copy-start.1
  0.7 0.7 copy-start

commit v2 on v1

--- a/solution.py
+++ b/solution.py
@@ -41,62 +41,67 @@
     return jnp.broadcast_to(value[row : row + 1, :], (8, BLOCK))
 
 
+def pairwise_sum(parts):
+    while len(parts) > 1:
+        parts = [sum(parts[i : i + 2][1:], parts[i]) for i in range(0, len(parts), 2)]
+    return parts[0]
+
+
 def inverse_factor(block):
     groups = BLOCK // 8
+    deep = STEP // 8
     sub = lax.broadcasted_iota(jnp.int32, (8, BLOCK), 0)
     lane = lax.broadcasted_iota(jnp.int32, (8, BLOCK), 1)
     unit = [jnp.where(sub == r, 1.0, 0.0).astype(F32) for r in range(8)]
     rows = [block[8 * g : 8 * g + 8, :] for g in range(groups)]
     result = []
-    for step in range(BLOCK // STEP):
-        first = step * STEP
+    for first in range(0, BLOCK, STEP):
         top = first // 8
         inside = (lane >= first) & (lane < first + STEP)
-        columns = [[lane_column(rows[top + a], first + c) for a in range(2)] for c in range(STEP)]
+        columns = [
+            [lane_column(rows[top + g], first + c) for g in range(deep)] for c in range(STEP)
+        ]
         pivot = [
-            jnp.where(inside, jnp.where(lane - first == sub + 8 * a, 1.0, 0.0), rows[top + a])
-            for a in range(2)
+            jnp.where(inside, jnp.where(lane - first == sub + 8 * g, 1.0, 0.0), rows[top + g])
+            for g in range(deep)
         ]
-        done = [jnp.zeros((8, BLOCK), F32), jnp.zeros((8, BLOCK), F32)]
-        for pair in range(STEP // 2):
-            c0, c1 = 2 * pair, 2 * pair + 1
+        done = [jnp.zeros((8, BLOCK), F32) for _ in range(deep)]
+        for c0 in range(0, STEP, 2):
+            c1 = c0 + 1
             a, r0, r1 = c0 // 8, c0 % 8, c1 % 8
             d00 = sublane_row(columns[c0][a], r0)
             d01 = sublane_row(columns[c1][a], r0)
             d11 = sublane_row(columns[c1][a], r1)
             scale = 1.0 / (d00 * d11 - d01 * d01)
-            w0 = [columns[c0][g] - unit[r0] if g == a else columns[c0][g] for g in range(2)]
-            w1 = [columns[c1][g] - unit[r1] if g == a else columns[c1][g] for g in range(2)]
-
-            def sweep(z):
-                z0, z1 = sublane_row(z[a], r0), sublane_row(z[a], r1)
-                y0 = (d11 * z0 - d01 * z1) * scale
-                y1 = (d00 * z1 - d01 * z0) * scale
-                return [z[g] - (w0[g] * y0 + w1[g] * y1) for g in range(2)], z0, z1
-
+            w0 = [columns[c0][g] - unit[r0] if g == a else columns[c0][g] for g in range(deep)]
+            w1 = [columns[c1][g] - unit[r1] if g == a else columns[c1][g] for g in range(deep)]
+            m0 = [(d11 * columns[c0][g] - d01 * columns[c1][g]) * scale for g in range(a, deep)]
+            m1 = [(d00 * columns[c1][g] - d01 * columns[c0][g]) * scale for g in range(a, deep)]
             for c in range(c1 + 1, STEP):
-                columns[c], _, _ = sweep(columns[c])
-            pivot, z0, z1 = sweep(pivot)
+                y0 = sublane_row(m0[c // 8 - a], c % 8)
+                y1 = sublane_row(m1[c // 8 - a], c % 8)
+                columns[c] = [columns[c][g] - (w0[g] * y0 + w1[g] * y1) for g in range(deep)]
+            z0, z1 = sublane_row(pivot[a], r0), sublane_row(pivot[a], r1)
+            y0 = (d11 * z0 - d01 * z1) * scale
+            y1 = (d00 * z1 - d01 * z0) * scale
+            pivot = [pivot[g] - (w0[g] * y0 + w1[g] * y1) for g in range(deep)]
             ratio = d01 / d00
             x0 = z0 * lax.rsqrt(d00)
             x1 = (z1 - z0 * ratio) * lax.rsqrt(d11 - d01 * ratio)
             done[a] = jnp.where(sub == r0, x0, jnp.where(sub == r1, x1, done[a]))
         result += done
-        if step == BLOCK // STEP - 1:
+        if first + STEP == BLOCK:
             break
-        near = range(top + 2, top + 4)
         old = list(rows)
-        for h in near:
-            total = jnp.where(inside, 0.0, old[h])
+        for h in range(top + deep, top + 2 * deep):
             parts = [
                 lane_column(old[h], first + c) * sublane_row(pivot[c // 8], c % 8)
                 for c in range(STEP)
             ]
-            while len(parts) > 1:
-                parts = [parts[i] + parts[i + 1] for i in range(0, len(parts), 2)]
-            rows[h] = total - parts[0]
-        if top + 4 < groups:
-            below = jnp.concatenate(old[top + 4 :], axis=0)
+            rows[h] = jnp.where(inside, 0.0, old[h]) - pairwise_sum(parts)
+        far = top + 2 * deep
+        if far < groups:
+            below = jnp.concatenate(old[far:], axis=0)
             spread = jnp.concatenate(
                 ([jnp.zeros((first, BLOCK), F32)] if first else [])
                 + pivot
@@ -104,9 +109,9 @@
                 axis=0,
             )
             change = dot_nn(below, spread, HIGH)
-            for h in range(top + 4, groups):
-                k = h - top - 4
-                rows[h] = jnp.where(inside, 0.0, old[h]) - change[8 * k : 8 * k + 8, :]
+            for h in range(far, groups):
+                k = 8 * (h - far)
+                rows[h] = jnp.where(inside, 0.0, old[h]) - change[k : k + 8, :]
     out = jnp.concatenate(result, axis=0)
     r = lax.broadcasted_iota(jnp.int32, (BLOCK, BLOCK), 0)
     c = lax.broadcasted_iota(jnp.int32, (BLOCK, BLOCK), 1)
@@ -158,7 +163,7 @@
         c = lax.broadcasted_iota(jnp.int32, (count, NB), 1)
         return r == c
 
-    chunk = 64
+    chunk = 256
 
     def fill_offdiagonal(row_slot, col_slot):
         @pl.loop(0, NB // chunk)
@@ -253,16 +258,16 @@
         for k in range(PANELS * parts):
             pl.when(index == k)(functools.partial(stage, k // parts, k % parts))
 
-    @pl.loop(0, 3)
-    def _(k):
-        slot = 2 + k
-        place = pl.ds(pl.multiple_of(k * NB, NB), NB)
-        fill_offdiagonal(slot, 0)
-        solved = solve(cov[...], 0)
+    @pl.loop(0, 3 * NB // chunk)
+    def _(i):
+        start = pl.multiple_of(2 * NB + i * chunk, chunk)
+        place = pl.ds(pl.multiple_of(i * chunk, chunk), chunk)
+        decay, gain = covariance(start, chunk, 0)
+        solved = solve((decay * gain).astype(BF16), 0)
         panels[0, place, :] = solved
-        fill_offdiagonal(slot, 1)
-        reduced = (cov[...].astype(F32) - dot_nt(solved, first_panel[...])).astype(BF16)
-        panels[1, place, :] = solve(reduced, 1)
+        decay, gain = covariance(start, chunk, NB)
+        value = (decay * gain).astype(BF16).astype(F32) - dot_nt(solved, first_panel[...])
+        panels[1, place, :] = solve(value.astype(BF16), 1)
 
     for k in range(2):
         tile = ids[3 + k]
@@ -275,14 +280,14 @@
         def _():
             col_place = pl.ds((1 + k) * NB, NB)
 
-            @pl.loop(0, NB // BLOCK)
+            @pl.loop(0, NB // chunk)
             def _(i):
-                start = pl.multiple_of(i * BLOCK, BLOCK)
+                start = pl.multiple_of(i * chunk, chunk)
                 decay, gain = covariance(
-                    pl.multiple_of(2 * NB + start, BLOCK), BLOCK, (3 + k) * NB
+                    pl.multiple_of(2 * NB + start, chunk), chunk, (3 + k) * NB
                 )
                 held = tile == row_tile
-                decay = jnp.where(own_pairs(start, BLOCK) & held, decay + NUGGET, decay)
+                decay = jnp.where(own_pairs(start, chunk) & held, decay + NUGGET, decay)
                 value = decay * gain
 
                 def kept(v):
@@ -290,9 +295,9 @@
 
                 value = kept(value)
                 for panel in range(PANELS):
-                    change = dot_nt(panels[panel, pl.ds(start, BLOCK), :], panels[panel, col_place, :])
+                    change = dot_nt(panels[panel, pl.ds(start, chunk), :], panels[panel, col_place, :])
                     value = kept(value - change)
-                out_ref[k, pl.ds(start, BLOCK), :] = value.astype(BF16)
+                out_ref[k, pl.ds(start, chunk), :] = value.astype(BF16)
 
     for panel in range(PANELS):
 

time: 89.3 us -> 79.1 us (0.89); the launches traced: 88.2 us -> 79 us
  Pallas kernels: 46.5 us -> 37.2 us
    pallas_call x1, Pallas kernels: 46.5 us -> 37.2 us  [device_tiles(): pl.pallas_call(tile_kernel, out_shape=jax.ShapeDtypeStruct((2, NB, NB), B...]
where the time goes in v2:
time: 79.1 us; the launch traced here: 79 us
  blocking collectives  38.3 us (48%)
  Pallas kernels  37.2 us (47%)
  local copies, waits for them, and re-layouts  3.35 us (4%)
    all_gather x1, blocking collectives, per_device(): gathered = lax.all_gather(own, 'row', axis=0, tiled=True)  38.3 us
    pallas_call x1, Pallas kernels, device_tiles(): pl.pallas_call(tile_kernel, out_shape=jax.ShapeDtypeStruct((2, NB, NB), B...  37.2 us
    broadcast_in_dim x1, local copies, waits for them, and re-layouts, per_device(): return jnp.transpose(tiles, (1, 0, 2))[None]  2.05 us

profile of v2, /device:TPU:1, one launch (start us, length us, event | category | flops | bytes accessed | tf_op | source)
XLA Modules:
  0.0 79.0 jit_solution(15281867803808272266)
XLA Ops:
  0.0 0.0 copy-start.2
  0.0 0.0 copy-start.1
  0.0 0.1 pad_add_fusion.place_ref
  0.1 0.6 copy-done.2
  0.7 0.0 copy-done.1
  0.7 0.0 copy-start
  0.7 0.7 copy-done
  1.4 38.3 %all_gather.3.gathered_ref = f32[32,3,512]{2,1,0:T(4,128)S(1)} all-gather(f32[1,3,512]{2,1,0:T(4,128)S(1)} %pad_maximum_fusion), channel_id=1, replica_groups=mesh['row'=32,'col'=16] {'row'}, dimensions={0}, use_global_device_ids=true | all-gather | bytes 202752 | tf_op jit(solution)/shard_map/all_gather | solution.py:345
  39.7 37.2 %shard_map.37 = bf16[2,512,512]{2,1,0:T(8,128)(2,1)S(1)} custom-call(s32[3]{0:T(128)S(1)} %pad_add_fusion.place_ref, f32[32,3,512]{2,1,0:T(4,128)S(1)} %all_gather.3.gathered_ref), custom_call_target="tpu_custom_call" | custom-call | tf_op jit(solution)/shard_map/pallas_call | solution.py:317
  76.9 2.0 %copy.5 = bf16[1,512,2,512]{3,2,1,0:T(2,128)(2,1)} copy(bf16[1,512,2,512]{3,1,2,0:T(8,128)(2,1)S(1)} %bitcast.11) | data formatting | bytes 2097152 | tf_op jit(solution)/shard_map/broadcast_in_dim | solution.py:348
  (2 shorter events, 0.0 us)
Async XLA Ops:
  0.0 0.7 copy-start.2
  0.0 0.7 copy-start.1
  0.7 0.7 copy-start

commit v3 on v2

--- a/solution.py
+++ b/solution.py
@@ -16,6 +16,7 @@
 TIME_RANGE = 8.0
 NUGGET = 1.0
 LOG2E = 1.4426950408889634
+MID_TIME = 1024.0
 HIGH = lax.Precision.HIGH
 F32 = jnp.float32
 BF16 = jnp.bfloat16
@@ -120,8 +121,8 @@
 
 def tile_kernel(
     place_ref, gathered_ref, out_ref,
-    lanes, subs, schur, lower, inverse, high, low, current, unit_inverse, factors,
-    first_panel, cov, panels,
+    lanes, subs, schur, lower, high, low, current, unit_inverse, pending,
+    first_panel, next_panel, next_diagonal, covs, panels,
 ):
     row_tile = place_ref[0]
     col_tile = place_ref[1]
@@ -139,9 +140,10 @@
         step = LOG2E / (RANGE_LENGTH * GRID)
         x = across.astype(F32) * step
         y = upward.astype(F32) * step
-        t = raw[1:2, :] * (LOG2E / TIME_RANGE)
+        t = (raw[1:2, :] - MID_TIME) * (LOG2E / TIME_RANGE)
         s = raw[2:3, :]
-        stacked = jnp.concatenate([x, y, t, s, jnp.zeros((4, NB), F32)], axis=0)
+        level = jnp.log(s) * LOG2E
+        stacked = jnp.concatenate([x, y, t, s, level + t, level - t, x, y], axis=0)
         lanes[:, slot * NB : (slot + 1) * NB] = stacked
         for q in range(NB // BLOCK):
             part = stacked[:, q * BLOCK : (q + 1) * BLOCK]
@@ -165,27 +167,20 @@
 
     chunk = 256
 
-    def fill_offdiagonal(row_slot, col_slot):
-        @pl.loop(0, NB // chunk)
-        def _(i):
-            start = pl.multiple_of(i * chunk, chunk)
-            decay, gain = covariance(
-                pl.multiple_of(row_slot * NB + start, chunk), chunk, col_slot * NB
-            )
-            cov[pl.ds(start, chunk), :] = (decay * gain).astype(BF16)
-
-    def fill_diagonal(slot, change):
-        @pl.loop(0, NB // chunk)
-        def _(i):
-            start = pl.multiple_of(i * chunk, chunk)
-            decay, gain = covariance(
-                pl.multiple_of(slot * NB + start, chunk), chunk, slot * NB
-            )
-            decay = jnp.where(own_pairs(start, chunk), decay + NUGGET, decay)
-            value = decay * gain
-            if change:
-                value = value - schur[pl.ds(start, chunk), :]
-            schur[pl.ds(start, chunk), :] = value
+    def diagonal_rows(slot, start, count):
+        decay, gain = covariance(slot * NB + start, count, slot * NB)
+        return jnp.where(own_pairs(start, count), decay + NUGGET, decay) * gain
+
+    def offdiagonal_rows(start, count, col_slot):
+        rows = pl.ds(start, count)
+        cols = pl.ds(col_slot * NB, NB)
+        dx = subs[rows, 0:1] - lanes[0:1, cols]
+        dy = subs[rows, 1:2] - lanes[1:2, cols]
+        square = dx * dx + dy * dy
+        level = jnp.minimum(
+            subs[rows, 5:6] + lanes[4:5, cols], subs[rows, 4:5] + lanes[5:6, cols]
+        )
+        return jnp.exp2(level - square * lax.rsqrt(square)).astype(BF16)
 
     def solve(values, panel):
         half = NB // 2
@@ -196,78 +191,85 @@
         ]
         return jnp.concatenate(parts, axis=1).astype(BF16)
 
-    fill_diagonal(0, False)
-    current[...] = schur[0:BLOCK, 0:BLOCK]
-    factors[...] = jnp.zeros_like(factors)
+    @pl.loop(0, NB // chunk)
+    def _(i):
+        start = pl.multiple_of(i * chunk, chunk)
+        schur[pl.ds(start, chunk), :] = diagonal_rows(0, start, chunk)
+
+    current[0, 0] = schur[0:BLOCK, 0:BLOCK]
+    lower[...] = jnp.zeros_like(lower)
+    high[...] = jnp.zeros_like(high)
+    low[...] = jnp.zeros_like(low)
     is_factor = (row_tile == col_tile) & (row_tile < PANELS)
 
     def stage(panel, part):
         begin, end = part * BLOCK, (part + 1) * BLOCK
-        inv = unit_inverse[...]
-        inverse[begin:end, begin:end] = inv
-
-        @pl.when(is_factor & (row_tile == panel))
-        def _():
-            factors[begin:end, begin:end] = dot_nt(current[...], inv, HIGH).astype(BF16)
+        inv = unit_inverse[panel, part]
+        rest = [-dot_nn(inv, pending[:, :begin], HIGH)] if part else []
+        if end < NB:
+            rest = rest + [inv, jnp.zeros((BLOCK, NB - end), F32)]
+        else:
+            rest = rest + [inv]
+        row = jnp.concatenate(rest, axis=1)
+        head = row.astype(BF16)
+        high[panel, begin:end, :] = head
+        low[panel, begin:end, :] = (row - head.astype(F32)).astype(BF16)
 
         if end < NB:
             solved = dot_nt(schur[end:, begin:end], inv, HIGH)
-            lower[end:, begin:end] = solved
-
-            @pl.when(is_factor & (row_tile == panel))
-            def _():
-                factors[end:, begin:end] = solved.astype(BF16)
+            lower[panel, end:, begin:end] = solved
 
             top = solved[:BLOCK]
-            current[...] = schur[end : end + BLOCK, end : end + BLOCK] - dot_nt(top, top, HIGH)
+            current[panel, part + 1] = schur[end : end + BLOCK, end : end + BLOCK] - dot_nt(top, top, HIGH)
             for q in range(end, NB, BLOCK):
                 here = solved[q - end : q - end + BLOCK]
                 schur[q:, q : q + BLOCK] = schur[q:, q : q + BLOCK] - dot_nt(
                     solved[q - end :], here, HIGH
                 )
         else:
-            half = NB // 2
-            for q in (0, half):
-                m = q + BLOCK
-                e = q + half
-                inverse[m:e, q:m] = -dot_nn(
-                    inverse[m:e, m:e], dot_nn(lower[m:e, q:m], inverse[q:m, q:m], HIGH), HIGH
-                )
-                inverse[q:m, m:e] = jnp.zeros((BLOCK, BLOCK), F32)
-            inverse[half:, :half] = -dot_nn(
-                inverse[half:, half:], dot_nn(lower[half:, :half], inverse[:half, :half], HIGH), HIGH
-            )
-            inverse[:half, half:] = jnp.zeros((half, half), F32)
-            whole = inverse[...]
-            head = whole.astype(BF16)
-            high[panel] = head
-            low[panel] = (whole - head.astype(F32)).astype(BF16)
             if panel + 1 < PANELS:
-                fill_offdiagonal(1, 0)
-                solved = solve(cov[...], 0)
+                solved = solve(next_panel[...], 0)
                 first_panel[...] = solved
-                schur[...] = dot_nt(solved, solved)
-                fill_diagonal(1, True)
-                current[...] = schur[0:BLOCK, 0:BLOCK]
+                current[panel + 1, 0] = next_diagonal[:BLOCK, :BLOCK] - dot_nt(solved[:BLOCK], solved[:BLOCK])
+                schur[...] = next_diagonal[...] - dot_nt(solved, solved)
+
+    def fill_pending(index, panel):
+        row = lower[panel, index * BLOCK : (index + 1) * BLOCK, :]
+        head = row.astype(BF16)
+        tail = (row - head.astype(F32)).astype(BF16)
+        both = jnp.concatenate([head, tail], axis=0)
+        product = dot_nn(both, high[panel])
+        pending[...] = product[:BLOCK] + product[BLOCK:] + dot_nn(head, low[panel])
 
     parts = NB // BLOCK
-
-    @pl.loop(0, PANELS * parts)
-    def _(index):
-        unit_inverse[...] = inverse_factor(current[...])
-        for k in range(PANELS * parts):
-            pl.when(index == k)(functools.partial(stage, k // parts, k % parts))
+    share = 3 * NB // parts
+
+    for index in range(parts):
+        near = pl.ds(index * BLOCK, BLOCK)
+        start = index * BLOCK
+        next_panel[near, :] = offdiagonal_rows(NB + start, BLOCK, 0)
+        next_diagonal[near, :] = diagonal_rows(1, start, BLOCK)
+        own = index * share
+        for panel in range(PANELS):
+            covs[panel, pl.ds(own, share), :] = offdiagonal_rows(2 * NB + own, share, panel)
+        fill_pending(index, 0)
+        unit_inverse[0, index] = inverse_factor(current[0, index])
+        stage(0, index)
+
+    for index in range(parts):
+        own = pl.ds(index * share, share)
+        solved = solve(covs[0, own, :], 0)
+        panels[0, own, :] = solved
+        change = dot_nt(solved, first_panel[...])
+        covs[1, own, :] = (covs[1, own, :].astype(F32) - change).astype(BF16)
+        fill_pending(index, 1)
+        unit_inverse[1, index] = inverse_factor(current[1, index])
+        stage(1, index)
 
     @pl.loop(0, 3 * NB // chunk)
     def _(i):
-        start = pl.multiple_of(2 * NB + i * chunk, chunk)
         place = pl.ds(pl.multiple_of(i * chunk, chunk), chunk)
-        decay, gain = covariance(start, chunk, 0)
-        solved = solve((decay * gain).astype(BF16), 0)
-        panels[0, place, :] = solved
-        decay, gain = covariance(start, chunk, NB)
-        value = (decay * gain).astype(BF16).astype(F32) - dot_nt(solved, first_panel[...])
-        panels[1, place, :] = solve(value.astype(BF16), 1)
+        panels[1, place, :] = solve(covs[1, place, :], 1)
 
     for k in range(2):
         tile = ids[3 + k]
@@ -276,28 +278,26 @@
         def _():
             out_ref[k] = jnp.zeros((NB, NB), BF16)
 
-        @pl.when((row_tile >= PANELS) & (tile >= PANELS))
-        def _():
+        def update(held):
             col_place = pl.ds((1 + k) * NB, NB)
 
             @pl.loop(0, NB // chunk)
             def _(i):
                 start = pl.multiple_of(i * chunk, chunk)
-                decay, gain = covariance(
-                    pl.multiple_of(2 * NB + start, chunk), chunk, (3 + k) * NB
-                )
-                held = tile == row_tile
-                decay = jnp.where(own_pairs(start, chunk) & held, decay + NUGGET, decay)
-                value = decay * gain
-
-                def kept(v):
-                    return jnp.where(held, v, v.astype(BF16).astype(F32))
-
-                value = kept(value)
+                place = pl.ds(start, chunk)
+                if held:
+                    value = diagonal_rows(2, start, chunk)
+                else:
+                    value = offdiagonal_rows(2 * NB + start, chunk, 3 + k).astype(F32)
                 for panel in range(PANELS):
-                    change = dot_nt(panels[panel, pl.ds(start, chunk), :], panels[panel, col_place, :])
-                    value = kept(value - change)
-                out_ref[k, pl.ds(start, chunk), :] = value.astype(BF16)
+                    value = value - dot_nt(panels[panel, place, :], panels[panel, col_place, :])
+                    if not held:
+                        value = value.astype(BF16).astype(F32)
+                out_ref[k, place, :] = value.astype(BF16)
+
+        inner = (row_tile >= PANELS) & (tile >= PANELS)
+        pl.when(inner & (tile == row_tile))(functools.partial(update, True))
+        pl.when(inner & (tile != row_tile))(functools.partial(update, False))
 
     for panel in range(PANELS):
 
@@ -305,11 +305,17 @@
         def _():
             out_ref[0] = panels[panel, 0:NB, :]
 
-    @pl.when(is_factor)
-    def _():
-        r = lax.broadcasted_iota(jnp.int32, (NB, NB), 0)
-        c = lax.broadcasted_iota(jnp.int32, (NB, NB), 1)
-        out_ref[0] = jnp.where(c <= r, factors[...].astype(F32), 0.0).astype(BF16)
+    for panel in range(PANELS):
+
+        @pl.when(is_factor & (row_tile == panel))
+        def _():
+            out_ref[0] = lower[panel].astype(BF16)
+            for p in range(parts):
+                span = slice(p * BLOCK, (p + 1) * BLOCK)
+                block = dot_nt(current[panel, p], unit_inverse[panel, p], HIGH)
+                r = lax.broadcasted_iota(jnp.int32, (BLOCK, BLOCK), 0)
+                c = lax.broadcasted_iota(jnp.int32, (BLOCK, BLOCK), 1)
+                out_ref[0, span, span] = jnp.where(c <= r, block, 0.0).astype(BF16)
 
 
 def device_tiles(place, gathered):
@@ -323,15 +329,16 @@
             pltpu.VMEM((8, 5 * NB), F32),
             pltpu.VMEM((5 * NB, 8), F32),
             pltpu.VMEM((NB, NB), F32),
-            pltpu.VMEM((NB, NB), F32),
-            pltpu.VMEM((NB, NB), F32),
+            pltpu.VMEM((PANELS, NB, NB), F32),
             pltpu.VMEM((PANELS, NB, NB), BF16),
             pltpu.VMEM((PANELS, NB, NB), BF16),
-            pltpu.VMEM((BLOCK, BLOCK), F32),
-            pltpu.VMEM((BLOCK, BLOCK), F32),
+            pltpu.VMEM((PANELS, NB // BLOCK, BLOCK, BLOCK), F32),
+            pltpu.VMEM((PANELS, NB // BLOCK, BLOCK, BLOCK), F32),
+            pltpu.VMEM((BLOCK, NB), F32),
             pltpu.VMEM((NB, NB), BF16),
             pltpu.VMEM((NB, NB), BF16),
-            pltpu.VMEM((NB, NB), BF16),
+            pltpu.VMEM((NB, NB), F32),
+            pltpu.VMEM((PANELS, 3 * NB, NB), BF16),
             pltpu.VMEM((PANELS, 3 * NB, NB), BF16),
         ],
         compiler_params=pltpu.CompilerParams(vmem_limit_bytes=48 * 1024 * 1024),

time: 79.1 us -> 73.7 us (0.932)
  Pallas kernels: 37.2 us -> 31.9 us
    pallas_call x1, Pallas kernels: 37.2 us -> 31.9 us  [device_tiles(): pl.pallas_call(tile_kernel, out_shape=jax.ShapeDtypeStruct((2, NB, NB), B...]
where the time goes in v3:
time: 73.7 us; the launch traced here: 73.6 us
  blocking collectives  38.3 us (52%)
  Pallas kernels  31.9 us (43%)
  local copies, waits for them, and re-layouts  3.35 us (5%)
    all_gather x1, blocking collectives, per_device(): gathered = lax.all_gather(own, 'row', axis=0, tiled=True)  38.3 us
    pallas_call x1, Pallas kernels, device_tiles(): pl.pallas_call(tile_kernel, out_shape=jax.ShapeDtypeStruct((2, NB, NB), B...  31.9 us
    broadcast_in_dim x1, local copies, waits for them, and re-layouts, per_device(): return jnp.transpose(tiles, (1, 0, 2))[None]  2.05 us

profile of v3, /device:TPU:1, one launch (start us, length us, event | category | flops | bytes accessed | tf_op | source)
XLA Modules:
  0.0 73.6 jit_solution(9030063277464230353)
XLA Ops:
  0.0 0.0 copy-start.2
  0.0 0.0 copy-start.1
  0.0 0.1 pad_add_fusion.place_ref
  0.1 0.6 copy-done.2
  0.7 0.0 copy-done.1
  0.7 0.0 copy-start
  0.7 0.7 copy-done
  1.4 38.3 %all_gather.3.gathered_ref = f32[32,3,512]{2,1,0:T(4,128)S(1)} all-gather(f32[1,3,512]{2,1,0:T(4,128)S(1)} %pad_maximum_fusion), channel_id=1, replica_groups=mesh['row'=32,'col'=16] {'row'}, dimensions={0}, use_global_device_ids=true | all-gather | bytes 202752 | tf_op jit(solution)/shard_map/all_gather | solution.py:352
  39.7 31.9 %shard_map.37 = bf16[2,512,512]{2,1,0:T(8,128)(2,1)S(1)} custom-call(s32[3]{0:T(128)S(1)} %pad_add_fusion.place_ref, f32[32,3,512]{2,1,0:T(4,128)S(1)} %all_gather.3.gathered_ref), custom_call_target="tpu_custom_call" | custom-call | tf_op jit(solution)/shard_map/pallas_call | solution.py:323
  71.6 2.0 %copy.5 = bf16[1,512,2,512]{3,2,1,0:T(2,128)(2,1)} copy(bf16[1,512,2,512]{3,1,2,0:T(8,128)(2,1)S(1)} %bitcast.11) | data formatting | bytes 2097152 | tf_op jit(solution)/shard_map/broadcast_in_dim | solution.py:355
  (2 shorter events, 0.0 us)
Async XLA Ops:
  0.0 0.7 copy-start.2
  0.0 0.7 copy-start.1
  0.7 0.7 copy-start

commit v4 on v3

--- a/solution.py
+++ b/solution.py
@@ -5,6 +5,7 @@
 from jax import lax
 from jax.experimental import pallas as pl
 from jax.experimental.pallas import tpu as pltpu
+from jax.sharding import Mesh
 from jax.sharding import PartitionSpec as P
 
 NB = 512
@@ -122,15 +123,84 @@
 def tile_kernel(
     place_ref, gathered_ref, out_ref,
     lanes, subs, schur, lower, high, low, current, unit_inverse, pending,
-    first_panel, next_panel, next_diagonal, covs, panels,
+    first_panel, next_panel, next_diagonal, partial, covs, panels,
 ):
     row_tile = place_ref[0]
     col_tile = place_ref[1]
     second_col = place_ref[2]
+    core = place_ref[3]
     ids = (0, 1, row_tile, col_tile, second_col)
 
-    for slot, tile in enumerate(ids):
-        raw = gathered_ref[tile]
+    def covariance(row_start, row_count, col_start):
+        rows = pl.ds(row_start, row_count)
+        cols = pl.ds(col_start, NB)
+        dx = subs[rows, 0:1] - lanes[0:1, cols]
+        dy = subs[rows, 1:2] - lanes[1:2, cols]
+        dt = subs[rows, 2:3] - lanes[2:3, cols]
+        square = dx * dx + dy * dy
+        length = square * lax.rsqrt(jnp.maximum(square, 1e-30))
+        decay = jnp.exp2(-(length + jnp.abs(dt)))
+        return decay, subs[rows, 3:4] * lanes[3:4, cols]
+
+    def own_pairs(start, count):
+        r = lax.broadcasted_iota(jnp.int32, (count, NB), 0) + start
+        c = lax.broadcasted_iota(jnp.int32, (count, NB), 1)
+        return r == c
+
+    chunk = 256
+
+    def diagonal_rows(slot, start, count):
+        decay, gain = covariance(slot * NB + start, count, slot * NB)
+        return jnp.where(own_pairs(start, count), decay + NUGGET, decay) * gain
+
+    def offdiagonal_rows(start, count, col_slot):
+        rows = pl.ds(start, count)
+        cols = pl.ds(col_slot * NB, NB)
+        dx = subs[rows, 0:1] - lanes[0:1, cols]
+        dy = subs[rows, 1:2] - lanes[1:2, cols]
+        square = dx * dx + dy * dy
+        level = jnp.minimum(
+            subs[rows, 5:6] + lanes[4:5, cols], subs[rows, 4:5] + lanes[5:6, cols]
+        )
+        return jnp.exp2(level - square * lax.rsqrt(square)).astype(BF16)
+
+    half = NB // 2
+
+    def half_solve(values, panel, begin):
+        span, depth = slice(begin, begin + half), slice(0, begin + half)
+        return dot_nt(values, high[panel, span, depth]) + dot_nt(values, low[panel, span, depth])
+
+    def solve(values, panel):
+        parts = [half_solve(values[:, :half], panel, 0), half_solve(values, panel, half)]
+        return jnp.concatenate(parts, axis=1).astype(BF16)
+
+    def diagonal_rows(slot, start, count):
+        decay, gain = covariance(slot * NB + start, count, slot * NB)
+        return jnp.where(own_pairs(start, count), decay + NUGGET, decay) * gain
+
+    def offdiagonal_rows(start, count, col_slot):
+        rows = pl.ds(start, count)
+        cols = pl.ds(col_slot * NB, NB)
+        dx = subs[rows, 0:1] - lanes[0:1, cols]
+        dy = subs[rows, 1:2] - lanes[1:2, cols]
+        square = dx * dx + dy * dy
+        level = jnp.minimum(
+            subs[rows, 5:6] + lanes[4:5, cols], subs[rows, 4:5] + lanes[5:6, cols]
+        )
+        return jnp.exp2(level - square * lax.rsqrt(square)).astype(BF16)
+
+    def solve(values, panel):
+        half = NB // 2
+        left = values[:, :half]
+        parts = [
+            dot_nt(left, high[panel, :half, :half]) + dot_nt(left, low[panel, :half, :half]),
+            dot_nt(values, high[panel, half:, :]) + dot_nt(values, low[panel, half:, :]),
+        ]
+        return jnp.concatenate(parts, axis=1).astype(BF16)
+
+    def prepare(slot, tile):
+        low_bit = lax.rem(tile, 2) if slot > 1 else tile % 2
+        raw = gathered_ref[tile - low_bit + jnp.bitwise_xor(low_bit, core)]
         codes = raw[0:1, :].astype(jnp.int32)
         across = jnp.zeros_like(codes)
         upward = jnp.zeros_like(codes)
@@ -149,54 +219,13 @@
             part = stacked[:, q * BLOCK : (q + 1) * BLOCK]
             subs[slot * NB + q * BLOCK : slot * NB + (q + 1) * BLOCK, :] = part.T
 
-    def covariance(row_start, row_count, col_start):
-        rows = pl.ds(row_start, row_count)
-        cols = pl.ds(col_start, NB)
-        dx = subs[rows, 0:1] - lanes[0:1, cols]
-        dy = subs[rows, 1:2] - lanes[1:2, cols]
-        dt = subs[rows, 2:3] - lanes[2:3, cols]
-        square = dx * dx + dy * dy
-        length = square * lax.rsqrt(jnp.maximum(square, 1e-30))
-        decay = jnp.exp2(-(length + jnp.abs(dt)))
-        return decay, subs[rows, 3:4] * lanes[3:4, cols]
-
-    def own_pairs(start, count):
-        r = lax.broadcasted_iota(jnp.int32, (count, NB), 0) + start
-        c = lax.broadcasted_iota(jnp.int32, (count, NB), 1)
-        return r == c
-
-    chunk = 256
-
-    def diagonal_rows(slot, start, count):
-        decay, gain = covariance(slot * NB + start, count, slot * NB)
-        return jnp.where(own_pairs(start, count), decay + NUGGET, decay) * gain
-
-    def offdiagonal_rows(start, count, col_slot):
-        rows = pl.ds(start, count)
-        cols = pl.ds(col_slot * NB, NB)
-        dx = subs[rows, 0:1] - lanes[0:1, cols]
-        dy = subs[rows, 1:2] - lanes[1:2, cols]
-        square = dx * dx + dy * dy
-        level = jnp.minimum(
-            subs[rows, 5:6] + lanes[4:5, cols], subs[rows, 4:5] + lanes[5:6, cols]
-        )
-        return jnp.exp2(level - square * lax.rsqrt(square)).astype(BF16)
-
-    def solve(values, panel):
-        half = NB // 2
-        left = values[:, :half]
-        parts = [
-            dot_nt(left, high[panel, :half, :half]) + dot_nt(left, low[panel, :half, :half]),
-            dot_nt(values, high[panel, half:, :]) + dot_nt(values, low[panel, half:, :]),
-        ]
-        return jnp.concatenate(parts, axis=1).astype(BF16)
-
-    @pl.loop(0, NB // chunk)
-    def _(i):
-        start = pl.multiple_of(i * chunk, chunk)
-        schur[pl.ds(start, chunk), :] = diagonal_rows(0, start, chunk)
+    prepare(0, 0)
+    for start in range(0, NB, chunk):
+        schur[start : start + chunk, :] = diagonal_rows(0, start, chunk)
 
     current[0, 0] = schur[0:BLOCK, 0:BLOCK]
+    for slot in range(1, 5):
+        prepare(slot, ids[slot])
     lower[...] = jnp.zeros_like(lower)
     high[...] = jnp.zeros_like(high)
     low[...] = jnp.zeros_like(low)
@@ -241,6 +270,9 @@
         product = dot_nn(both, high[panel])
         pending[...] = product[:BLOCK] + product[BLOCK:] + dot_nn(head, low[panel])
 
+    def kept(k, value):
+        return jnp.where(ids[3 + k] == row_tile, value, value.astype(BF16).astype(F32))
+
     parts = NB // BLOCK
     share = 3 * NB // parts
 
@@ -257,19 +289,27 @@
         stage(0, index)
 
     for index in range(parts):
-        own = pl.ds(index * share, share)
-        solved = solve(covs[0, own, :], 0)
-        panels[0, own, :] = solved
-        change = dot_nt(solved, first_panel[...])
-        covs[1, own, :] = (covs[1, own, :].astype(F32) - change).astype(BF16)
+        if index < 2:
+            same = ids[3 + index] == row_tile
+            decay, gain = covariance(2 * NB, NB, (3 + index) * NB)
+            decay = jnp.where(own_pairs(0, NB) & same, decay + NUGGET, decay)
+            partial[index] = kept(index, decay * gain)
+        if index < 3:
+            own = pl.ds(index * NB, NB)
+            solved = solve(covs[0, own, :], 0)
+            panels[0, own, :] = solved
+            change = dot_nt(solved, first_panel[...])
+            covs[1, own, :] = (covs[1, own, :].astype(F32) - change).astype(BF16)
+        else:
+            panels[1, :, :half] = half_solve(covs[1, :, :half], 1, 0).astype(BF16)
+            for k in range(2):
+                change = dot_nt(panels[0, :NB, :], panels[0, (1 + k) * NB : (2 + k) * NB, :])
+                partial[k] = kept(k, partial[k] - change)
         fill_pending(index, 1)
         unit_inverse[1, index] = inverse_factor(current[1, index])
         stage(1, index)
 
-    @pl.loop(0, 3 * NB // chunk)
-    def _(i):
-        place = pl.ds(pl.multiple_of(i * chunk, chunk), chunk)
-        panels[1, place, :] = solve(covs[1, place, :], 1)
+    panels[1, :, half:] = half_solve(covs[1], 1, half).astype(BF16)
 
     for k in range(2):
         tile = ids[3 + k]
@@ -278,26 +318,10 @@
         def _():
             out_ref[k] = jnp.zeros((NB, NB), BF16)
 
-        def update(held):
-            col_place = pl.ds((1 + k) * NB, NB)
-
-            @pl.loop(0, NB // chunk)
-            def _(i):
-                start = pl.multiple_of(i * chunk, chunk)
-                place = pl.ds(start, chunk)
-                if held:
-                    value = diagonal_rows(2, start, chunk)
-                else:
-                    value = offdiagonal_rows(2 * NB + start, chunk, 3 + k).astype(F32)
-                for panel in range(PANELS):
-                    value = value - dot_nt(panels[panel, place, :], panels[panel, col_place, :])
-                    if not held:
-                        value = value.astype(BF16).astype(F32)
-                out_ref[k, place, :] = value.astype(BF16)
-
-        inner = (row_tile >= PANELS) & (tile >= PANELS)
-        pl.when(inner & (tile == row_tile))(functools.partial(update, True))
-        pl.when(inner & (tile != row_tile))(functools.partial(update, False))
+        @pl.when((row_tile >= PANELS) & (tile >= PANELS))
+        def _():
+            change = dot_nt(panels[1, :NB, :], panels[1, (1 + k) * NB : (2 + k) * NB, :])
+            out_ref[k] = (partial[k] - change).astype(BF16)
 
     for panel in range(PANELS):
 
@@ -338,6 +362,7 @@
             pltpu.VMEM((NB, NB), BF16),
             pltpu.VMEM((NB, NB), BF16),
             pltpu.VMEM((NB, NB), F32),
+            pltpu.VMEM((2, NB, NB), F32),
             pltpu.VMEM((PANELS, 3 * NB, NB), BF16),
             pltpu.VMEM((PANELS, 3 * NB, NB), BF16),
         ],
@@ -346,20 +371,29 @@
 
 
 def per_device(locations, scales, sample_times):
-    row_place = lax.axis_index("row")
+    core = lax.axis_index("core")
+    row_place = lax.axis_index("chip") * 2 + core
     col_place = lax.axis_index("col")
+    chips = lax.axis_size("chip")
     own = jnp.stack([locations.astype(F32), sample_times.astype(F32), scales], axis=1)
-    gathered = lax.all_gather(own, "row", axis=0, tiled=True)
-    place = jnp.stack([row_place, col_place, col_place + lax.axis_size("col")]).astype(jnp.int32)
-    tiles = device_tiles(place, gathered)
+    other = lax.ppermute(own, "core", [(0, 1), (1, 0)])
+    pair = jnp.concatenate([own, other], axis=0)
+    copies = jnp.broadcast_to(pair[None], (chips,) + pair.shape)
+    gathered = lax.all_to_all(copies, "chip", 0, 0, tiled=True)
+    gathered = gathered.reshape((2 * chips,) + own.shape[1:])
+    place = jnp.stack([row_place, col_place, col_place + lax.axis_size("col"), core])
+    tiles = device_tiles(place.astype(jnp.int32), gathered)
     return jnp.transpose(tiles, (1, 0, 2))[None]
 
 
 def solution(mesh):
+    rows, cols = mesh.devices.shape
+    split = Mesh(mesh.devices.reshape(rows // 2, 2, cols), ("chip", "core", "col"))
+    row = P(None, ("chip", "core"))
     return jax.shard_map(
         per_device,
-        mesh=mesh,
-        in_specs=(P(None, "row"), P(None, "row"), P(None, "row")),
-        out_specs=P(None, "row", None, "col"),
+        mesh=split,
+        in_specs=(row, row, row),
+        out_specs=P(None, ("chip", "core"), None, "col"),
         check_vma=False,
     )

time: 73.7 us -> 71.5 us (0.970)
  the two profiles are of different devices: /device:TPU:1 before, /device:TPU:58 now
where the time goes in v4:
time: 71.5 us; the launch traced here: 71.2 us
  Pallas kernels  32.4 us (45%)
  waiting for transfers between devices  17.3 us (24%)
  starting transfers between devices  17.1 us (24%)
  local copies, waits for them, and re-layouts  3.53 us (5%)
  other arithmetic  0.8 us (1%)
    pallas_call x1, Pallas kernels, device_tiles(): pl.pallas_call(tile_kernel, out_shape=jax.ShapeDtypeStruct((2, NB, NB), B...  32.4 us
    all_to_all x1, waiting for transfers between devices, per_device(): gathered = lax.all_to_all(copies, 'chip', 0, 0, tiled=True)  16.2 us
    all_to_all x1, starting transfers between devices, per_device(): gathered = lax.all_to_all(copies, 'chip', 0, 0, tiled=True)  15.2 us
    broadcast_in_dim x1, local copies, waits for them, and re-layouts, per_device(): return jnp.transpose(tiles, (1, 0, 2))[None]  2.05 us
    ppermute x1, starting transfers between devices, per_device(): other = lax.ppermute(own, 'core', [(0, 1), (1, 0)])  1.91 us
  transfers between devices with their start and end apart: 2, of which 2 were waited for; matrix products, arithmetic and copies ran while one was open for 0% of the time, Pallas kernels for 0%

profile of v4, /device:TPU:58, one launch (start us, length us, event | category | flops | bytes accessed | tf_op | source)
XLA Modules:
  0.0 71.2 jit_solution(9210769587974006877)
XLA Ops:
  0.0 0.7 convert_bitcast_fusion
  0.7 0.0 copy-start
  0.7 0.7 copy-done
  1.4 1.9 %collective-permute-start = (f32[1,3,512]{2,0,1:T(1,128)S(1)}, f32[1,3,512]{2,0,1:T(1,128)S(1)}, u32[]{:S(2)}, u32[]{:S(2)}) collective-permute-start(f32[1,3,512]{2,0,1:T(1,128)S(1)} %pad_maximum_fusion.1), channel_id=1, source_target_pairs={{0,16},{16,0},{1,17},{17,1},{2,18},{18,2},{3,19},{19,3},{4,20},{20... | collective-permute-start | bytes 18440 | tf_op jit(solution)/shard_map/ppermute | solution.py:379
  3.3 1.1 %collective-permute-done = f32[1,3,512]{2,0,1:T(1,128)S(1)} collective-permute-done((f32[1,3,512]{2,0,1:T(1,128)S(1)}, f32[1,3,512]{2,0,1:T(1,128)S(1)}, u32[]{:S(2)}, u32[]{:S(2)}) %collective-permute-start) | collective-permute-done | bytes 6176 | tf_op jit(solution)/shard_map/ppermute | solution.py:379
  4.5 0.7 %broadcast_in_dim.4 = f32[16,2,3,512]{3,1,2,0:T(2,128)} broadcast(f32[2,3,512]{2,0,1:T(2,128)S(1)} %pad_maximum_fusion), dimensions={1,2,3} | broadcast | bytes 208896 | tf_op jit(solution)/shard_map/broadcast_in_dim | solution.py:381
  5.2 15.2 %all-to-all-start = ((f32[16,2,3,512]{3,1,2,0:T(2,128)}), f32[16,2,3,512]{3,1,2,0:T(2,128)S(1)}, u32[]{:S(2)}, u32[]{:S(2)}) async-start(f32[16,2,3,512]{3,1,2,0:T(2,128)} %broadcast_in_dim.4), calls=%async_computation | async-start | bytes 393216 | tf_op jit(solution)/shard_map/all_to_all | solution.py:382
  20.4 0.1 pad_add_fusion.place_ref
  20.5 16.2 %all-to-all-done = f32[16,2,3,512]{3,1,2,0:T(2,128)S(1)} async-done(((f32[16,2,3,512]{3,1,2,0:T(2,128)}), f32[16,2,3,512]{3,1,2,0:T(2,128)S(1)}, u32[]{:S(2)}, u32[]{:S(2)}) %all-to-all-start) | async-done | bytes 196640 | tf_op jit(solution)/shard_map/all_to_all | solution.py:382
  36.6 0.1 copy.5
  36.7 32.4 %shard_map.37 = bf16[2,512,512]{2,1,0:T(8,128)(2,1)S(1)} custom-call(s32[4]{0:T(128)S(1)} %pad_add_fusion.place_ref, f32[32,3,512]{2,1,0:T(4,128)S(1)} %bitcast.14), custom_call_target="tpu_custom_call" | custom-call | tf_op jit(solution)/shard_map/pallas_call | solution.py:347
  69.1 2.0 %copy.6 = bf16[1,512,2,512]{3,2,1,0:T(2,128)(2,1)} copy(bf16[1,512,2,512]{3,1,2,0:T(8,128)(2,1)S(1)} %bitcast.13) | data formatting | bytes 2097152 | tf_op jit(solution)/shard_map/broadcast_in_dim | solution.py:386
  (2 shorter events, 0.0 us)
Async XLA Ops:
  0.7 0.7 copy-start
  1.4 3.1 %collective-permute-start = (f32[1,3,512]{2,0,1:T(1,128)S(1)}, f32[1,3,512]{2,0,1:T(1,128)S(1)}, u32[]{:S(2)}, u32[]{:S(2)}) collective-permute-start(f32[1,3,512]{2,0,1:T(1,128)S(1)} %pad_maximum_fusion.1), channel_id=1, source_target_pairs={{0,16},{16,0},{1,17},{17,1},{2,18},{18,2},{3,19},{19,3},{4,20},{20... | collective-permute-start | bytes 18440 | tf_op jit(solution)/shard_map/ppermute | solution.py:379
  5.2 31.5 %all-to-all-start = ((f32[16,2,3,512]{3,1,2,0:T(2,128)}), f32[16,2,3,512]{3,1,2,0:T(2,128)S(1)}, u32[]{:S(2)}, u32[]{:S(2)}) async-start(f32[16,2,3,512]{3,1,2,0:T(2,128)} %broadcast_in_dim.4), calls=%async_computation | async-start | bytes 393216 | tf_op jit(solution)/shard_map/all_to_all | solution.py:382

commit v5 on v4

--- a/solution.py
+++ b/solution.py
@@ -316,37 +316,37 @@
 
         @pl.when((row_tile < PANELS) & (tile > row_tile))
         def _():
-            out_ref[k] = jnp.zeros((NB, NB), BF16)
+            out_ref[:, k, :] = jnp.zeros((NB, NB), BF16)
 
         @pl.when((row_tile >= PANELS) & (tile >= PANELS))
         def _():
             change = dot_nt(panels[1, :NB, :], panels[1, (1 + k) * NB : (2 + k) * NB, :])
-            out_ref[k] = (partial[k] - change).astype(BF16)
+            out_ref[:, k, :] = (partial[k] - change).astype(BF16)
 
     for panel in range(PANELS):
 
         @pl.when((col_tile == panel) & (row_tile > panel))
         def _():
-            out_ref[0] = panels[panel, 0:NB, :]
+            out_ref[:, 0, :] = panels[panel, 0:NB, :]
 
     for panel in range(PANELS):
 
         @pl.when(is_factor & (row_tile == panel))
         def _():
-            out_ref[0] = lower[panel].astype(BF16)
+            out_ref[:, 0, :] = lower[panel].astype(BF16)
             for p in range(parts):
                 span = slice(p * BLOCK, (p + 1) * BLOCK)
                 block = dot_nt(current[panel, p], unit_inverse[panel, p], HIGH)
                 r = lax.broadcasted_iota(jnp.int32, (BLOCK, BLOCK), 0)
                 c = lax.broadcasted_iota(jnp.int32, (BLOCK, BLOCK), 1)
-                out_ref[0, span, span] = jnp.where(c <= r, block, 0.0).astype(BF16)
+                out_ref[span, 0, span] = jnp.where(c <= r, block, 0.0).astype(BF16)
 
 
 def device_tiles(place, gathered):
     vmem = pl.BlockSpec(memory_space=pltpu.VMEM)
     return pl.pallas_call(
         tile_kernel,
-        out_shape=jax.ShapeDtypeStruct((2, NB, NB), BF16),
+        out_shape=jax.ShapeDtypeStruct((NB, 2, NB), BF16),
         in_specs=[pl.BlockSpec(memory_space=pltpu.SMEM), vmem],
         out_specs=vmem,
         scratch_shapes=[
@@ -375,7 +375,11 @@
     row_place = lax.axis_index("chip") * 2 + core
     col_place = lax.axis_index("col")
     chips = lax.axis_size("chip")
-    own = jnp.stack([locations.astype(F32), sample_times.astype(F32), scales], axis=1)
+    kind = lax.broadcasted_iota(jnp.int32, (1, 3, NB), 1)
+    codes, times = locations.astype(F32), sample_times.astype(F32)
+    own = jnp.where(
+        kind == 0, codes[:, None], jnp.where(kind == 1, times[:, None], scales[:, None])
+    )
     other = lax.ppermute(own, "core", [(0, 1), (1, 0)])
     pair = jnp.concatenate([own, other], axis=0)
     copies = jnp.broadcast_to(pair[None], (chips,) + pair.shape)
@@ -383,7 +387,7 @@
     gathered = gathered.reshape((2 * chips,) + own.shape[1:])
     place = jnp.stack([row_place, col_place, col_place + lax.axis_size("col"), core])
     tiles = device_tiles(place.astype(jnp.int32), gathered)
-    return jnp.transpose(tiles, (1, 0, 2))[None]
+    return tiles[None]
 
 
 def solution(mesh):

time: 71.5 us -> 70.8 us (level)
  the two profiles are of different devices: /device:TPU:58 before, /device:TPU:38 now
where the time goes in v5:
time: 70.8 us; the launch traced here: 70.5 us
  Pallas kernels  33.7 us (48%)
  waiting for transfers between devices  17.3 us (24%)
  starting transfers between devices  17.1 us (24%)
  local copies, waits for them, and re-layouts  1.48 us (2%)
  other arithmetic  0.87 us (1%)
    pallas_call x1, Pallas kernels, device_tiles(): pl.pallas_call(tile_kernel, out_shape=jax.ShapeDtypeStruct((NB, 2, NB), B...  33.7 us
    all_to_all x1, waiting for transfers between devices, per_device(): gathered = lax.all_to_all(copies, 'chip', 0, 0, tiled=True)  16.2 us
    all_to_all x1, starting transfers between devices, per_device(): gathered = lax.all_to_all(copies, 'chip', 0, 0, tiled=True)  15.2 us
    ppermute x1, starting transfers between devices, per_device(): other = lax.ppermute(own, 'core', [(0, 1), (1, 0)])  1.91 us
  transfers between devices with their start and end apart: 2, of which 2 were waited for; matrix products, arithmetic and copies ran while one was open for 0% of the time, Pallas kernels for 0%

profile of v5, /device:TPU:38, one launch (start us, length us, event | category | flops | bytes accessed | tf_op | source)
XLA Modules:
  0.0 70.5 jit_solution(3388520137283106)
XLA Ops:
  0.0 0.0 copy-start
  0.0 0.7 convert_element_type.6
  0.7 0.0 copy-done
  0.7 0.0 copy-start.1
  0.7 0.7 copy-done.1
  1.4 0.1 broadcast_select_fusion
  1.5 1.9 %collective-permute-start = (f32[1,3,512]{2,0,1:T(1,128)S(1)}, f32[1,3,512]{2,0,1:T(1,128)S(1)}, u32[]{:S(2)}, u32[]{:S(2)}) collective-permute-start(f32[1,3,512]{2,0,1:T(1,128)S(1)} %broadcast_select_fusion), channel_id=1, source_target_pairs={{0,16},{16,0},{1,17},{17,1},{2,18},{18,2},{3,19},{19,3},{4,20},{20... | collective-permute-start | bytes 18440 | tf_op jit(solution)/shard_map/ppermute | solution.py:383
  3.4 1.1 %collective-permute-done = f32[1,3,512]{2,0,1:T(1,128)S(1)} collective-permute-done((f32[1,3,512]{2,0,1:T(1,128)S(1)}, f32[1,3,512]{2,0,1:T(1,128)S(1)}, u32[]{:S(2)}, u32[]{:S(2)}) %collective-permute-start) | collective-permute-done | bytes 6176 | tf_op jit(solution)/shard_map/ppermute | solution.py:383
  4.5 0.7 %broadcast_in_dim.48 = f32[16,2,3,512]{3,1,2,0:T(2,128)} broadcast(f32[2,3,512]{2,0,1:T(2,128)S(1)} %pad_maximum_fusion), dimensions={1,2,3} | broadcast | bytes 208896 | tf_op jit(solution)/shard_map/broadcast_in_dim | solution.py:385
  5.3 15.2 %all-to-all-start = ((f32[16,2,3,512]{3,1,2,0:T(2,128)}), f32[16,2,3,512]{3,1,2,0:T(2,128)S(1)}, u32[]{:S(2)}, u32[]{:S(2)}) async-start(f32[16,2,3,512]{3,1,2,0:T(2,128)} %broadcast_in_dim.48), calls=%async_computation | async-start | bytes 393216 | tf_op jit(solution)/shard_map/all_to_all | solution.py:386
  20.5 0.1 pad_add_fusion.place_ref
  20.6 16.2 %all-to-all-done = f32[16,2,3,512]{3,1,2,0:T(2,128)S(1)} async-done(((f32[16,2,3,512]{3,1,2,0:T(2,128)}), f32[16,2,3,512]{3,1,2,0:T(2,128)S(1)}, u32[]{:S(2)}, u32[]{:S(2)}) %all-to-all-start) | async-done | bytes 196640 | tf_op jit(solution)/shard_map/all_to_all | solution.py:386
  36.7 0.1 copy.4
  36.8 33.7 %shard_map.37 = bf16[512,2,512]{2,1,0:T(2,128)(2,1)} custom-call(s32[4]{0:T(128)S(1)} %pad_add_fusion.place_ref, f32[32,3,512]{2,1,0:T(4,128)S(1)} %bitcast.9), custom_call_target="tpu_custom_call" | custom-call | tf_op jit(solution)/shard_map/pallas_call | solution.py:347
  (3 shorter events, 0.0 us)
Async XLA Ops:
  0.0 0.7 copy-start
  0.7 0.7 copy-start.1
  1.5 3.1 %collective-permute-start = (f32[1,3,512]{2,0,1:T(1,128)S(1)}, f32[1,3,512]{2,0,1:T(1,128)S(1)}, u32[]{:S(2)}, u32[]{:S(2)}) collective-permute-start(f32[1,3,512]{2,0,1:T(1,128)S(1)} %broadcast_select_fusion), channel_id=1, source_target_pairs={{0,16},{16,0},{1,17},{17,1},{2,18},{18,2},{3,19},{19,3},{4,20},{20... | collective-permute-start | bytes 18440 | tf_op jit(solution)/shard_map/ppermute | solution.py:383
  5.3 31.5 %all-to-all-start = ((f32[16,2,3,512]{3,1,2,0:T(2,128)}), f32[16,2,3,512]{3,1,2,0:T(2,128)S(1)}, u32[]{:S(2)}, u32[]{:S(2)}) async-start(f32[16,2,3,512]{3,1,2,0:T(2,128)} %broadcast_in_dim.48), calls=%async_computation | async-start | bytes 393216 | tf_op jit(solution)/shard_map/all_to_all | solution.py:386
